TPU v7x, 32 devices: a whole 2x2x4 slice. The times are simulated.
32 devices in a mesh: dp: 8 (over z, x), tensor: 4 (over y, core).
Axes of the slice: x: 2, y: 2, z: 4, core: 2. Of those that a mesh axis runs over, the one named last changes fastest.
Arguments:
- attn_out: bfloat16 [8192, 8192], P('dp', 'tensor'), may hold values from -8 to 8, as said below
- grad_out: bfloat16 [8192, 256], P('dp'), may hold values from -1.0080408 to 1.0080408, as said below
- grad_acc: float32 [256, 8192], P('dp', 'tensor'), may hold values from -1060 to 1060, as said below
- master_weight: float32 [256, 8192], P('dp', 'tensor'), may hold values from -60 to 60, as said below
- moment_m: float32 [256, 8192], P('dp', 'tensor'), may hold values from -4 to 4
- moment_v: float32 [256, 8192], P('dp', 'tensor'), may hold values from 0.001 to 0.01
Outputs:
- moment_new: float32 [256, 8192], P('dp', 'tensor')
- second_new: float32 [256, 8192], P('dp', 'tensor')
- scaled_step: float32 [256, 8192], P('dp', 'tensor')
Inputs may be any that keep to these rules, and one draw needn't show every extreme that they name: `attn_out`: finite values. `grad_out`: finite values. `grad_acc`: finite values. `master_weight`: finite values.
All inputs are finite; a program needn't handle non-finite values.
Results may differ from a plain program's by a relative error of at most 0.0003.
Values sent between devices are 32-bit elements; how exact they have to be, the bound alone decides.
A program may use at most 128 MiB of HBM per device.

v0:
```python
import jax
import jax.numpy as jnp
from jax import lax
from jax.sharding import PartitionSpec as P

beta_first = 0.9
beta_second = 0.999
weight_decay = 0.01
epsilon = 1e-06


def lamb_moments(gradient, divisor, weight, moment, second):
    clipped = gradient / divisor
    moment_new = beta_first * moment + (1.0 - beta_first) * clipped
    second_new = beta_second * second + (1.0 - beta_second) * clipped * clipped
    update = moment_new / (jnp.sqrt(second_new) + epsilon) + weight_decay * weight
    return (moment_new, second_new, update)


def shards(attn_out, grad_out, grad_acc, master_weight, moment_m, moment_v):
    entry_count = grad_out.shape[1] * attn_out.shape[1] * lax.axis_size("tensor")
    batch_grad = lax.psum_scatter(
        lax.dot_general(
            grad_out, attn_out, (((0,), (0,)), ((), ())), preferred_element_type=jnp.float32
        ),
        "dp",
        scatter_dimension=0,
        tiled=True,
    )
    gradient = grad_acc + batch_grad
    grad_whole, weight_whole, moment_whole, second_whole = (
        lax.all_to_all(gradient, "tensor", split_axis=0, concat_axis=1, tiled=True),
        lax.all_to_all(master_weight, "tensor", split_axis=0, concat_axis=1, tiled=True),
        lax.all_to_all(moment_m, "tensor", split_axis=0, concat_axis=1, tiled=True),
        lax.all_to_all(moment_v, "tensor", split_axis=0, concat_axis=1, tiled=True),
    )
    grad_energy = lax.psum(jnp.sum(grad_whole * grad_whole), ("dp", "tensor"))
    divisor = jnp.sqrt(grad_energy / entry_count + epsilon)
    moment_rows, second_rows, update = lamb_moments(
        grad_whole, divisor, weight_whole, moment_whole, second_whole
    )
    weight_norm = jnp.sqrt(jnp.sum(weight_whole * weight_whole, axis=1, keepdims=True))
    update_norm = jnp.sqrt(jnp.sum(update * update, axis=1, keepdims=True))
    step_rows = weight_norm / (update_norm + epsilon) * update
    moment_new, second_new, scaled_step = (
        lax.all_to_all(moment_rows, "tensor", split_axis=1, concat_axis=0, tiled=True),
        lax.all_to_all(second_rows, "tensor", split_axis=1, concat_axis=0, tiled=True),
        lax.all_to_all(step_rows, "tensor", split_axis=1, concat_axis=0, tiled=True),
    )
    return (moment_new, second_new, scaled_step)


def solution(mesh):
    in_specs = (
        P("dp", "tensor"),
        P("dp", None),
        P("dp", "tensor"),
        P("dp", "tensor"),
        P("dp", "tensor"),
        P("dp", "tensor"),
    )
    out_specs = (P("dp", "tensor"), P("dp", "tensor"), P("dp", "tensor"))
    return jax.shard_map(shards, mesh=mesh, in_specs=in_specs, out_specs=out_specs, check_vma=False)
```

profile of v0, /device:TPU:0, one launch (start us, length us, event | category | flops | bytes accessed | tf_op | source)
XLA Modules:
  0.0 176.4 jit_solution(820822908228714176)
XLA Ops:
  7.2 0.0 copy-start
  7.2 0.0 copy-start.2
  7.2 0.0 copy-start.1
  7.2 0.0 reduce-scatter.2.cloned.1.call-start
  7.2 1.0 copy-done
  8.2 4.8 %fusion.4 = f32[256,2048]{1,0:T(8,128)} fusion(bf16[1024,256]{1,0:T(8,128)(2,1)S(1)} %copy-done, bf16[1024,2048]{1,0:T(8,128)(2,1)} %param.6), kind=kOutput, calls=%fused_computation.12 | convolution fusion | flops 1073741824 | bytes 6815744 | tf_op jit(solution)/shard_map/dot_general | solution.py:23
  13.0 0.0 reduce-scatter.2.cloned.1.call-update
  13.0 0.0 copy-done.2
  13.1 10.1 %all_to_all.100 = f32[4,8,2048]{2,1,0:T(8,128)S(1)} all-to-all(f32[4,8,2048]{2,1,0:T(8,128)S(1)} %bitcast.35), channel_id=1, replica_groups=mesh['dp'=8,'tensor'=4] {'tensor'}, dimensions={0} | all-to-all | bytes 524288 | tf_op jit(solution)/shard_map/all_to_all | solution.py:33
  23.1 3.4 %all-to-all-start = ((f32[4,8,2048]{2,1,0:T(8,128)}), f32[4,8,2048]{2,1,0:T(8,128)S(1)}, u32[]{:S(2)}, u32[]{:S(2)}) async-start(f32[4,8,2048]{2,1,0:T(8,128)} %bitcast), calls=%async_computation | async-start | bytes 524288 | tf_op jit(solution)/shard_map/all_to_all | solution.py:34
  26.5 57.5 %reduce-scatter.2.cloned.1.call-done = f32[32,2048]{1,0:T(8,128)} async-done(((f32[256,2048]{1,0:T(8,128)}), f32[32,2048]{1,0:T(8,128)}) %reduce-scatter.2.cloned.1.call-update) | async-done | bytes 262160 | tf_op jit(solution)/shard_map/reduce_scatter | solution.py:22
  84.0 0.0 copy-done.1
  84.0 1.0 add_bitcast_fusion
  85.0 0.0 all-to-all-done
  85.0 8.6 %all_to_all.101 = f32[4,8,2048]{2,1,0:T(8,128)S(1)} all-to-all(f32[4,8,2048]{2,1,0:T(8,128)S(1)} %add_bitcast_fusion), channel_id=1, replica_groups=mesh['dp'=8,'tensor'=4] {'tensor'}, dimensions={0} | all-to-all | bytes 524288 | tf_op jit(solution)/shard_map/all_to_all | solution.py:32
  93.6 3.4 %all-to-all-start.3 = ((f32[4,8,2048]{2,1,0:T(8,128)}), f32[4,8,2048]{2,1,0:T(8,128)S(1)}, u32[]{:S(2)}, u32[]{:S(2)}) async-start(f32[4,8,2048]{2,1,0:T(8,128)} %bitcast.6), calls=%async_computation.4 | async-start | bytes 524288 | tf_op jit(solution)/shard_map/all_to_all | solution.py:35
  97.0 0.7 multiply_reduce_fusion.2
  97.7 0.2 multiply_reduce_fusion.1
  97.8 40.3 %psum.7 = f32[]{:T(128)} all-reduce(f32[]{:T(128)} %multiply_reduce_fusion.2), channel_id=1, replica_groups=mesh['dp'=8,'tensor'=4] {'dp','tensor'}, use_global_device_ids=true, to_apply=%region_2.0 | all-reduce | flops 1 | bytes 8 | tf_op jit(solution)/shard_map/psum | solution.py:37
  138.9 0.0 all-to-all-done.3
  138.9 1.0 multiply_reduce_fusion
  139.9 0.1 broadcast_multiply_fusion
  140.0 9.6 %all_to_all.102 = f32[8,4,2048]{2,0,1:T(8,128)S(1)} all-to-all(f32[8,4,2048]{2,0,1:T(8,128)S(1)} %broadcast_multiply_fusion), channel_id=1, replica_groups=mesh['dp'=8,'tensor'=4] {'tensor'}, dimensions={1} | all-to-all | bytes 524288 | tf_op jit(solution)/shard_map/all_to_all | solution.py:48
  149.6 8.4 %all_to_all.103 = f32[8,4,2048]{2,0,1:T(8,128)S(1)} all-to-all(f32[8,4,2048]{2,0,1:T(8,128)S(1)} %get-tuple-element.5), channel_id=1, replica_groups=mesh['dp'=8,'tensor'=4] {'tensor'}, dimensions={1} | all-to-all | bytes 524288 | tf_op jit(solution)/shard_map/all_to_all | solution.py:47
  158.0 3.4 %all-to-all-start.2 = ((f32[8,4,2048]{2,0,1:T(8,128)}), f32[8,4,2048]{2,0,1:T(8,128)S(1)}, u32[]{:S(2)}, u32[]{:S(2)}) async-start(f32[8,4,2048]{2,0,1:T(8,128)} %get-tuple-element.6), calls=%async_computation.3 | async-start | bytes 524288 | tf_op jit(solution)/shard_map/all_to_all | solution.py:46
  161.4 6.0 %all-to-all-done.2 = f32[8,4,2048]{2,0,1:T(8,128)S(1)} async-done(((f32[8,4,2048]{2,0,1:T(8,128)}), f32[8,4,2048]{2,0,1:T(8,128)S(1)}, u32[]{:S(2)}, u32[]{:S(2)}) %all-to-all-start.2) | async-done | bytes 262176 | tf_op jit(solution)/shard_map/all_to_all | solution.py:46
  167.4 0.7 copy.12
  168.1 0.7 copy.13
  168.8 0.7 copy.14
  (1 shorter events, 0.0 us)
Async XLA Ops:
  7.2 1.0 copy-start
  7.2 5.9 %copy-start.2 = (f32[32,2048]{1,0:T(8,128)S(1)}, f32[32,2048]{1,0:T(8,128)}, u32[]{:S(2)}) copy-start(f32[32,2048]{1,0:T(8,128)} %param.9) | copy-start | bytes 786436
  7.2 76.8 %copy-start.1 = (f32[32,2048]{1,0:T(8,128)S(1)}, f32[32,2048]{1,0:T(8,128)}, u32[]{:S(2)}) copy-start(f32[32,2048]{1,0:T(8,128)} %param.8) | copy-start | bytes 786436
  7.2 76.8 %reduce-scatter.2.cloned.1.call-start = ((), (), s32[]{:S(2)}) async-start(), calls=%async_computation.8 | async-start | bytes 2359296 | tf_op jit(solution)/shard_map/reduce_scatter | solution.py:22
  23.1 61.9 %all-to-all-start = ((f32[4,8,2048]{2,1,0:T(8,128)}), f32[4,8,2048]{2,1,0:T(8,128)S(1)}, u32[]{:S(2)}, u32[]{:S(2)}) async-start(f32[4,8,2048]{2,1,0:T(8,128)} %bitcast), calls=%async_computation | async-start | bytes 524288 | tf_op jit(solution)/shard_map/all_to_all | solution.py:34
  93.6 45.3 %all-to-all-start.3 = ((f32[4,8,2048]{2,1,0:T(8,128)}), f32[4,8,2048]{2,1,0:T(8,128)S(1)}, u32[]{:S(2)}, u32[]{:S(2)}) async-start(f32[4,8,2048]{2,1,0:T(8,128)} %bitcast.6), calls=%async_computation.4 | async-start | bytes 524288 | tf_op jit(solution)/shard_map/all_to_all | solution.py:35
  158.0 9.4 %all-to-all-start.2 = ((f32[8,4,2048]{2,0,1:T(8,128)}), f32[8,4,2048]{2,0,1:T(8,128)S(1)}, u32[]{:S(2)}, u32[]{:S(2)}) async-start(f32[8,4,2048]{2,0,1:T(8,128)} %get-tuple-element.6), calls=%async_computation.3 | async-start | bytes 524288 | tf_op jit(solution)/shard_map/all_to_all | solution.py:46
Sparse Core Ops, SparseCore 0:
  13.2 70.7 reduce-scatter.1
where the time goes:
time: 177 us; the launch traced here: 176 us
  blocking collectives  77 us (44%)
  waiting for transfers between devices  63.5 us (36%)
  between operations  14.8 us (8%)
  starting transfers between devices  10.3 us (6%)
  matrix products  4.81 us (3%)
  local copies, waits for them, and re-layouts  3.09 us (2%)
  other arithmetic  2.93 us (2%)
    reduce_scatter x1, waiting for transfers between devices, shards(): lax.psum_scatter(lax.dot_general(grad_out, attn_out, (((0,), (0,)), ((),...  57.5 us
    psum x1, blocking collectives, shards(): grad_energy = lax.psum(jnp.sum(grad_whole * grad_whole), ('dp', 'tensor'))  40.3 us
    all_to_all x1, blocking collectives, shards(): lax.all_to_all(master_weight, 'tensor', split_axis=0, concat_axis=1, tile...  10.1 us
    all_to_all x1, blocking collectives, shards(): lax.all_to_all(step_rows, 'tensor', split_axis=1, concat_axis=0, tiled=True)  9.57 us
    all_to_all x1, blocking collectives, shards(): lax.all_to_all(gradient, 'tensor', split_axis=0, concat_axis=1, tiled=True)  8.56 us
    all_to_all x1, blocking collectives, shards(): lax.all_to_all(second_rows, 'tensor', split_axis=1, concat_axis=0, tiled=...  8.41 us
    all_to_all x1, waiting for transfers between devices, shards(): lax.all_to_all(moment_rows, 'tensor', split_axis=1, concat_axis=0, tiled=...  6 us
    dot_general x1, matrix products, shards(): lax.dot_general(grad_out, attn_out, (((0,), (0,)), ((), ())), preferred_e...  4.81 us
  transfers between devices with their start and end apart: 4, of which 2 were waited for; matrix products, arithmetic and copies ran while one was open for 1% of the time, Pallas kernels for 0%

commit v1 on v0

v1 whole, which is shorter than its diff:
```python
import functools

import jax
import jax.numpy as jnp
from jax import lax
from jax.experimental import pallas as pl
from jax.experimental.pallas import tpu as pltpu
from jax.sharding import PartitionSpec as P

beta_first = 0.9
beta_second = 0.999
weight_decay = 0.01
epsilon = 1e-06

MESH = pl.DeviceIdType.MESH
CHUNKS = 4
AHEAD = 4
LANES = 128
MAX_LINE = 4


def lamb_moments(gradient, divisor, weight, moment, second):
    clipped = gradient / divisor
    moment_new = beta_first * moment + (1.0 - beta_first) * clipped
    second_new = beta_second * second + (1.0 - beta_second) * clipped * clipped
    update = moment_new / (jnp.sqrt(second_new) + epsilon) + weight_decay * weight
    return (moment_new, second_new, update)


def block_order(at, line):
    right = list(range(line - 1, at, -1))
    left = list(range(0, at))
    order = []
    while right or left:
        group = []
        if right and len(right) >= len(left):
            group.append(right.pop(0))
            if left and len(left) > len(right):
                group.append(left.pop(0))
        else:
            group.append(left.pop(0))
            if right and len(right) > len(left):
                group.append(right.pop(0))
        order += [(place, chunk) for chunk in range(CHUNKS) for place in group]
    return order + [(at, chunk) for chunk in range(CHUNKS)]


def lane_sums(values):
    total = values[:, :LANES]
    for at in range(LANES, values.shape[1], LANES):
        total = total + values[:, at : at + LANES]
    return total


def row_groups(values):
    total = values[:8]
    for at in range(8, values.shape[0], 8):
        total = total + values[at : at + 8]
    return total


def lamb_kernel(
    n_dp, n_tensor, entry_count,
    attn, grad_out, grad_acc, weight, moment, second,
    moment_out, second_out, step_out,
    a_buf, g_buf, gt_buf, part, pair_in, from_left, from_right,
    acc_buf, w_buf, m_buf, v_buf, grad_buf, mo_buf, so_buf, st_buf,
    wsum, usum, esum, tsum,
    load_sem, out_sem,
    pair_send, pair_recv, right_send, right_recv, left_send, left_recv,
    w_send, w_recv, u_send, u_recv, e_send, e_recv, t_send, t_recv,
):
    line = n_dp // 2
    dp = lax.axis_index("dp")
    tensor = lax.axis_index("tensor")
    place, side = dp // 2, dp % 2
    width = part.shape[3]

    loads = [pltpu.make_async_copy(grad_out, g_buf, load_sem.at[0])]
    for c in range(CHUNKS):
        loads.append(
            pltpu.make_async_copy(attn.at[:, pl.ds(c * width, width)], a_buf.at[c], load_sem.at[1 + c])
        )
    for i, (src, dst) in enumerate(((weight, w_buf), (grad_acc, acc_buf), (moment, m_buf), (second, v_buf))):
        loads.append(pltpu.make_async_copy(src, dst, load_sem.at[1 + CHUNKS + i]))
    for copy in loads:
        copy.start()

    dp_peer = [lax.rem(dp + k, n_dp) for k in range(n_dp)]
    tensor_peer = [lax.rem(tensor + k, n_tensor) for k in range(n_tensor)]

    barrier = pltpu.get_barrier_semaphore()
    for k in range(1, n_dp):
        pl.semaphore_signal(barrier, inc=1, device_id=(dp_peer[k], tensor), device_id_type=MESH)
    for k in range(1, n_tensor):
        pl.semaphore_signal(barrier, inc=1, device_id=(dp, tensor_peer[k]), device_id_type=MESH)

    def pair_copy(item):
        to, c = item
        i = to * CHUNKS + c
        return pltpu.make_async_remote_copy(
            src_ref=part.at[2 * to + (1 - side), c], dst_ref=pair_in.at[to, c],
            send_sem=pair_send.at[i], recv_sem=pair_recv.at[i],
            device_id=(2 * place + (1 - side), tensor), device_id_type=MESH,
        )

    def line_copy(item, step):
        to, c = item
        i = to * CHUNKS + c
        into, send, recv = (from_left, right_send, right_recv) if step > 0 else (from_right, left_send, left_recv)
        return pltpu.make_async_remote_copy(
            src_ref=part.at[2 * to + side, c], dst_ref=into.at[to, c],
            send_sem=send.at[i], recv_sem=recv.at[i],
            device_id=(dp + 2 * step, tensor), device_id_type=MESH,
        )

    def tensor_copy(k, src, dst, send, recv):
        return pltpu.make_async_remote_copy(
            src_ref=src, dst_ref=dst.at[k], send_sem=send.at[k], recv_sem=recv.at[k],
            device_id=(dp, tensor_peer[k]), device_id_type=MESH,
        )

    def dp_copy(k, src, dst, send, recv):
        return pltpu.make_async_remote_copy(
            src_ref=src, dst_ref=dst.at[k], send_sem=send.at[k], recv_sem=recv.at[k],
            device_id=(dp_peer[k], tensor), device_id_type=MESH,
        )

    loads[0].wait()
    gt_buf[...] = g_buf[...].T

    orders = [block_order(at, line) for at in range(line)]
    for c in range(CHUNKS):
        loads[1 + c].wait()
        product = jnp.dot(gt_buf[...], a_buf[c], preferred_element_type=jnp.float32)
        part[:, c] = product.reshape(n_dp, product.shape[0] // n_dp, width)
        if c == 0:
            pl.semaphore_wait(barrier, n_dp + n_tensor - 2)
        for at in range(line):
            @pl.when(place == at)
            def _(at=at, c=c):
                for item in orders[at][:AHEAD]:
                    if item[1] == c:
                        pair_copy(item).start()

    loads[1 + CHUNKS].wait()
    wsum[0] = lane_sums(jnp.square(w_buf[...]))
    w_copies = [tensor_copy(k, wsum.at[0], wsum, w_send, w_recv) for k in range(1, n_tensor)]
    for copy in w_copies:
        copy.start()
    for i in range(1, 4):
        loads[1 + CHUNKS + i].wait()

    for at in range(line):
        @pl.when(place == at)
        def _(at=at):
            order = orders[at]
            energy = jnp.zeros((8, LANES), jnp.float32)
            for i, item in enumerate(order):
                to, c = item
                pair_copy(item).wait_recv()
                if i + AHEAD < len(order):
                    pair_copy(order[i + AHEAD]).start()
                total = part[2 * to + side, c] + pair_in[to, c]
                if at > 0 and to >= at:
                    line_copy(item, 1).wait_recv()
                    total = total + from_left[to, c]
                if at < line - 1 and to <= at:
                    line_copy(item, -1).wait_recv()
                    total = total + from_right[to, c]
                if to != at:
                    part[2 * to + side, c] = total
                    line_copy(item, 1 if to > at else -1).start()
                else:
                    total = total + acc_buf[:, c * width : (c + 1) * width]
                    grad_buf[:, c * width : (c + 1) * width] = total
                    energy = energy + row_groups(lane_sums(jnp.square(total)))
            tsum[0] = energy

    t_copies = [tensor_copy(k, tsum.at[0], tsum, t_send, t_recv) for k in range(1, n_tensor)]
    for copy in t_copies:
        copy.start()
    energy = tsum[0]
    for k, copy in enumerate(t_copies):
        copy.wait_recv()
        energy = energy + tsum[k + 1]
    esum[0] = energy
    e_copies = [dp_copy(k, esum.at[0], esum, e_send, e_recv) for k in range(1, n_dp)]
    for copy in e_copies:
        copy.start()
    for k, copy in enumerate(e_copies):
        copy.wait_recv()
        energy = energy + esum[k + 1]
    mean_square = jnp.sum(energy, keepdims=True) * (1.0 / entry_count)
    divisor = jnp.sqrt(mean_square + epsilon)

    moment_new, second_new, update = lamb_moments(grad_buf[...], divisor, w_buf[...], m_buf[...], v_buf[...])
    st_buf[...] = update
    usum[0] = lane_sums(update * update)
    u_copies = [tensor_copy(k, usum.at[0], usum, u_send, u_recv) for k in range(1, n_tensor)]
    for copy in u_copies:
        copy.start()
    mo_buf[...] = moment_new
    so_buf[...] = second_new
    outs = [
        pltpu.make_async_copy(mo_buf, moment_out, out_sem.at[0]),
        pltpu.make_async_copy(so_buf, second_out, out_sem.at[1]),
        pltpu.make_async_copy(st_buf, step_out, out_sem.at[2]),
    ]
    outs[0].start()
    outs[1].start()
    weight_square = wsum[0]
    for k, copy in enumerate(w_copies):
        copy.wait_recv()
        weight_square = weight_square + wsum[k + 1]
    weight_norm = jnp.sqrt(jnp.sum(weight_square, axis=1, keepdims=True))
    update_square = usum[0]
    for k, copy in enumerate(u_copies):
        copy.wait_recv()
        update_square = update_square + usum[k + 1]
    update_norm = jnp.sqrt(jnp.sum(update_square, axis=1, keepdims=True))
    st_buf[...] = weight_norm / (update_norm + epsilon) * st_buf[...]
    outs[2].start()

    for copy in w_copies + t_copies + e_copies + u_copies:
        copy.wait_send()
    for at in range(line):
        @pl.when(place == at)
        def _(at=at):
            for item in orders[at]:
                pair_copy(item).wait_send()
                if item[0] != at:
                    line_copy(item, 1 if item[0] > at else -1).wait_send()
    for copy in outs:
        copy.wait()


def kernel_shards(n_dp, n_tensor, attn_out, grad_out, grad_acc, master_weight, moment_m, moment_v):
    tokens, columns = attn_out.shape
    rows_all = grad_out.shape[1]
    rows = rows_all // n_dp
    line = n_dp // 2
    width = columns // CHUNKS
    f32 = jnp.float32
    items = line * CHUNKS
    dma = pltpu.SemaphoreType.DMA
    whole = lambda: pltpu.VMEM((rows, columns), f32)
    out = jax.ShapeDtypeStruct((rows, columns), f32)
    return pl.pallas_call(
        functools.partial(lamb_kernel, n_dp, n_tensor, rows_all * columns * n_tensor),
        out_shape=(out, out, out),
        in_specs=[pl.BlockSpec(memory_space=pl.ANY)] * 6,
        out_specs=[pl.BlockSpec(memory_space=pl.ANY)] * 3,
        scratch_shapes=[
            pltpu.VMEM((CHUNKS, tokens, width), jnp.bfloat16),
            pltpu.VMEM((tokens, rows_all), jnp.bfloat16),
            pltpu.VMEM((rows_all, tokens), jnp.bfloat16),
            pltpu.VMEM((n_dp, CHUNKS, rows, width), f32),
            pltpu.VMEM((line, CHUNKS, rows, width), f32),
            pltpu.VMEM((line, CHUNKS, rows, width), f32),
            pltpu.VMEM((line, CHUNKS, rows, width), f32),
            whole(), whole(), whole(), whole(), whole(), whole(), whole(), whole(),
            pltpu.VMEM((n_tensor, rows, LANES), f32),
            pltpu.VMEM((n_tensor, rows, LANES), f32),
            pltpu.VMEM((n_dp, 8, LANES), f32),
            pltpu.VMEM((n_tensor, 8, LANES), f32),
            dma((CHUNKS + 5,)), dma((3,)),
            dma((items,)), dma((items,)), dma((items,)), dma((items,)), dma((items,)), dma((items,)),
            dma((n_tensor,)), dma((n_tensor,)), dma((n_tensor,)), dma((n_tensor,)),
            dma((n_dp,)), dma((n_dp,)), dma((n_tensor,)), dma((n_tensor,)),
        ],
        compiler_params=pltpu.CompilerParams(
            collective_id=0, has_side_effects=True, vmem_limit_bytes=40 * 2**20
        ),
        name="lamb_step",
    )(attn_out, grad_out, grad_acc, master_weight, moment_m, moment_v)


def collective_shards(n_dp, n_tensor, attn_out, grad_out, grad_acc, master_weight, moment_m, moment_v):
    entry_count = grad_out.shape[1] * attn_out.shape[1] * n_tensor
    batch_grad = lax.psum_scatter(
        lax.dot_general(
            grad_out, attn_out, (((0,), (0,)), ((), ())), preferred_element_type=jnp.float32
        ),
        "dp",
        scatter_dimension=0,
        tiled=True,
    )
    gradient = grad_acc + batch_grad
    grad_energy = lax.psum(jnp.sum(gradient * gradient), ("dp", "tensor"))
    divisor = jnp.sqrt(grad_energy / entry_count + epsilon)
    moment_new, second_new, update = lamb_moments(gradient, divisor, master_weight, moment_m, moment_v)
    squares = jnp.stack([jnp.sum(master_weight * master_weight, axis=1), jnp.sum(update * update, axis=1)])
    weight_norm, update_norm = jnp.sqrt(lax.psum(squares, "tensor"))
    return (moment_new, second_new, (weight_norm / (update_norm + epsilon))[:, None] * update)


def solution(mesh):
    n_dp, n_tensor = mesh.shape["dp"], mesh.shape["tensor"]
    fits = n_dp % 2 == 0 and 2 <= n_dp // 2 <= MAX_LINE
    shards = functools.partial(kernel_shards if fits else collective_shards, n_dp, n_tensor)
    split = P("dp", "tensor")
    in_specs = (split, P("dp", None), split, split, split, split)
    return jax.shard_map(shards, mesh=mesh, in_specs=in_specs, out_specs=(split,) * 3, check_vma=False)
```

time: 177 us -> 51.4 us (0.29)
  blocking collectives: 77 us -> 0 us
  waiting for transfers between devices: 63.5 us -> 0 us
  Pallas kernels: 0 us -> 41.3 us
  between operations: 14.8 us -> 0.65 us
  starting transfers between devices: 10.3 us -> 0 us
  local copies, waits for them, and re-layouts: 3.09 us -> 9.13 us
  matrix products: 4.81 us -> 0 us
  other arithmetic: 2.93 us -> 0 us
    reduce_scatter x1 -> x0, waiting for transfers between devices: 57.5 us -> none  [shards(): lax.psum_scatter(lax.dot_general(grad_out, attn_out, (((0,), (0,)), ((),...]
    pallas_call x0 -> x1, Pallas kernels: none -> 41.3 us  [kernel_shards(): pl.pallas_call(functools.partial(lamb_kernel, n_dp, n_tensor, rows_all *...]
    psum x1 -> x0, blocking collectives: 40.3 us -> none  [shards(): grad_energy = lax.psum(jnp.sum(grad_whole * grad_whole), ('dp', 'tensor'))]
    all_to_all x4 -> x0, blocking collectives: 36.6 us -> none  [the longest x1 10.1 us: shards(): lax.all_to_all(master_weight, 'tensor', split_axis=0, concat_axis=1, tile...]
    all_to_all x3 -> x0, starting transfers between devices: 10.2 us -> none  [the longest x1 3.41 us: shards(): lax.all_to_all(moment_m, 'tensor', split_axis=0, concat_axis=1, tiled=True)]
    unnamed x9 -> x15, local copies, waits for them, and re-layouts: 3.09 us -> 9.13 us
    all_to_all x3 -> x0, waiting for transfers between devices: 6.01 us -> none  [the longest x1 6 us: shards(): lax.all_to_all(moment_rows, 'tensor', split_axis=1, concat_axis=0, tiled=...]
    dot_general x1 -> x0, matrix products: 4.81 us -> none  [shards(): lax.dot_general(grad_out, attn_out, (((0,), (0,)), ((), ())), preferred_e...]
  transfers between devices with their start and end apart: 4 -> 0, of which waited for: 2 -> 0; matrix products, arithmetic and copies ran while one was open for 1% -> 0% of each run, Pallas kernels for 0% -> 0%
where the time goes in v1:
time: 51.4 us; the launch traced here: 51.1 us
  Pallas kernels  41.3 us (80%)
  local copies, waits for them, and re-layouts  9.13 us (18%)
  between operations  0.65 us (1%)
    pallas_call x1, Pallas kernels, kernel_shards(): pl.pallas_call(functools.partial(lamb_kernel, n_dp, n_tensor, rows_all *...  41.3 us
    unnamed x15, local copies, waits for them, and re-layouts  9.13 us

profile of v1, /device:TPU:0, one launch (start us, length us, event | category | flops | bytes accessed | tf_op | source)
XLA Modules:
  0.0 51.1 jit_solution(4559869536210077282)
XLA Ops:
  0.6 0.0 copy-start
  0.6 2.2 %copy-done = bf16[1024,2048]{1,0:T(8,128)(2,1)S(1)} copy-done((bf16[1024,2048]{1,0:T(8,128)(2,1)S(1)}, bf16[1024,2048]{1,0:T(8,128)(2,1)}, u32[]{:S(2)}) %copy-start) | copy-done | bytes 4194328
  2.8 0.0 copy-start.1
  2.8 1.0 %copy-done.1 = bf16[1024,256]{1,0:T(8,128)(2,1)S(1)} copy-done((bf16[1024,256]{1,0:T(8,128)(2,1)S(1)}, bf16[1024,256]{1,0:T(8,128)(2,1)}, u32[]{:S(2)}) %copy-start.1) | copy-done | bytes 524312
  3.9 0.0 copy-start.2
  3.9 0.9 %copy-done.2 = f32[32,2048]{1,0:T(8,128)S(1)} copy-done((f32[32,2048]{1,0:T(8,128)S(1)}, f32[32,2048]{1,0:T(8,128)}, u32[]{:S(2)}) %copy-start.2) | copy-done | bytes 262168
  4.8 0.0 copy-start.3
  4.8 0.9 %copy-done.3 = f32[32,2048]{1,0:T(8,128)S(1)} copy-done((f32[32,2048]{1,0:T(8,128)S(1)}, f32[32,2048]{1,0:T(8,128)}, u32[]{:S(2)}) %copy-start.3) | copy-done | bytes 262168
  5.8 0.0 copy-start.4
  5.8 0.9 %copy-done.4 = f32[32,2048]{1,0:T(8,128)S(1)} copy-done((f32[32,2048]{1,0:T(8,128)S(1)}, f32[32,2048]{1,0:T(8,128)}, u32[]{:S(2)}) %copy-start.4) | copy-done | bytes 262168
  6.7 0.0 copy-start.5
  6.7 0.9 %copy-done.5 = f32[32,2048]{1,0:T(8,128)S(1)} copy-done((f32[32,2048]{1,0:T(8,128)S(1)}, f32[32,2048]{1,0:T(8,128)}, u32[]{:S(2)}) %copy-start.5) | copy-done | bytes 262168
  7.7 41.3 %lamb_step.1 = (f32[32,2048]{1,0:T(8,128)S(1)}, f32[32,2048]{1,0:T(8,128)S(1)}, f32[32,2048]{1,0:T(8,128)S(1)}) custom-call(bf16[1024,2048]{1,0:T(8,128)(2,1)S(1)} %copy-done, bf16[1024,256]{1,0:T(8,128)(2,1)S(1)} %copy-done.1, f32[32,2048]{1,0:T(8,128)S(1)} %copy-done.2, f32[32,2048]{1,0:T(8,128)S(1)} %copy-done.3, f32[32,2048]{1,0:T(8,128)S(1)} %copy-done.4, ...), custom_call_target="tpu_custom_call" | custom-call | tf_op jit(solution)/shard_map/lamb_step/pallas_call | solution.py:249
  49.0 0.7 %copy.12 = f32[32,2048]{1,0:T(8,128)} copy(f32[32,2048]{1,0:T(8,128)S(1)} %get-tuple-element.6) | data formatting | bytes 524288
  49.7 0.7 %copy.13 = f32[32,2048]{1,0:T(8,128)} copy(f32[32,2048]{1,0:T(8,128)S(1)} %get-tuple-element.7) | data formatting | bytes 524288
  50.4 0.7 %copy.14 = f32[32,2048]{1,0:T(8,128)} copy(f32[32,2048]{1,0:T(8,128)S(1)} %get-tuple-element.8) | data formatting | bytes 524288
Async XLA Ops:
  0.6 2.2 %copy-start = (bf16[1024,2048]{1,0:T(8,128)(2,1)S(1)}, bf16[1024,2048]{1,0:T(8,128)(2,1)}, u32[]{:S(2)}) copy-start(bf16[1024,2048]{1,0:T(8,128)(2,1)} %attn.1) | copy-start | bytes 12582916
  2.8 1.0 %copy-start.1 = (bf16[1024,256]{1,0:T(8,128)(2,1)S(1)}, bf16[1024,256]{1,0:T(8,128)(2,1)}, u32[]{:S(2)}) copy-start(bf16[1024,256]{1,0:T(8,128)(2,1)} %grad_out.1) | copy-start | bytes 1572868
  3.9 0.9 %copy-start.2 = (f32[32,2048]{1,0:T(8,128)S(1)}, f32[32,2048]{1,0:T(8,128)}, u32[]{:S(2)}) copy-start(f32[32,2048]{1,0:T(8,128)} %grad_acc.1) | copy-start | bytes 786436
  4.8 0.9 %copy-start.3 = (f32[32,2048]{1,0:T(8,128)S(1)}, f32[32,2048]{1,0:T(8,128)}, u32[]{:S(2)}) copy-start(f32[32,2048]{1,0:T(8,128)} %weight.1) | copy-start | bytes 786436
  5.8 0.9 %copy-start.4 = (f32[32,2048]{1,0:T(8,128)S(1)}, f32[32,2048]{1,0:T(8,128)}, u32[]{:S(2)}) copy-start(f32[32,2048]{1,0:T(8,128)} %moment.1) | copy-start | bytes 786436
  6.7 0.9 %copy-start.5 = (f32[32,2048]{1,0:T(8,128)S(1)}, f32[32,2048]{1,0:T(8,128)}, u32[]{:S(2)}) copy-start(f32[32,2048]{1,0:T(8,128)} %second.1) | copy-start | bytes 786436

commit v2 on v1

--- a/solution.py
+++ b/solution.py
@@ -62,9 +62,9 @@
 def lamb_kernel(
     n_dp, n_tensor, entry_count,
     attn, grad_out, grad_acc, weight, moment, second,
-    moment_out, second_out, step_out,
+    grad_out_ref, divisor_out, trust_out,
     a_buf, g_buf, gt_buf, part, pair_in, from_left, from_right,
-    acc_buf, w_buf, m_buf, v_buf, grad_buf, mo_buf, so_buf, st_buf,
+    acc_buf, w_buf, m_buf, v_buf, grad_buf, div_buf, trust_buf,
     wsum, usum, esum, tsum,
     load_sem, out_sem,
     pair_send, pair_recv, right_send, right_recv, left_send, left_recv,
@@ -177,9 +177,15 @@
                     energy = energy + row_groups(lane_sums(jnp.square(total)))
             tsum[0] = energy
 
+    outs = [
+        pltpu.make_async_copy(grad_buf, grad_out_ref, out_sem.at[0]),
+        pltpu.make_async_copy(div_buf, divisor_out, out_sem.at[1]),
+        pltpu.make_async_copy(trust_buf, trust_out, out_sem.at[2]),
+    ]
     t_copies = [tensor_copy(k, tsum.at[0], tsum, t_send, t_recv) for k in range(1, n_tensor)]
     for copy in t_copies:
         copy.start()
+    outs[0].start()
     energy = tsum[0]
     for k, copy in enumerate(t_copies):
         copy.wait_recv()
@@ -194,21 +200,13 @@
     mean_square = jnp.sum(energy, keepdims=True) * (1.0 / entry_count)
     divisor = jnp.sqrt(mean_square + epsilon)
 
-    moment_new, second_new, update = lamb_moments(grad_buf[...], divisor, w_buf[...], m_buf[...], v_buf[...])
-    st_buf[...] = update
+    div_buf[...] = jnp.broadcast_to(divisor, div_buf.shape)
+    outs[1].start()
+    update = lamb_moments(grad_buf[...], divisor, w_buf[...], m_buf[...], v_buf[...])[2]
     usum[0] = lane_sums(update * update)
     u_copies = [tensor_copy(k, usum.at[0], usum, u_send, u_recv) for k in range(1, n_tensor)]
     for copy in u_copies:
         copy.start()
-    mo_buf[...] = moment_new
-    so_buf[...] = second_new
-    outs = [
-        pltpu.make_async_copy(mo_buf, moment_out, out_sem.at[0]),
-        pltpu.make_async_copy(so_buf, second_out, out_sem.at[1]),
-        pltpu.make_async_copy(st_buf, step_out, out_sem.at[2]),
-    ]
-    outs[0].start()
-    outs[1].start()
     weight_square = wsum[0]
     for k, copy in enumerate(w_copies):
         copy.wait_recv()
@@ -219,7 +217,7 @@
         copy.wait_recv()
         update_square = update_square + usum[k + 1]
     update_norm = jnp.sqrt(jnp.sum(update_square, axis=1, keepdims=True))
-    st_buf[...] = weight_norm / (update_norm + epsilon) * st_buf[...]
+    trust_buf[...] = jnp.broadcast_to(weight_norm / (update_norm + epsilon), trust_buf.shape)
     outs[2].start()
 
     for copy in w_copies + t_copies + e_copies + u_copies:
@@ -235,6 +233,15 @@
         copy.wait()
 
 
+def result_kernel(gradient, divisor, trust, weight, moment, second, moment_out, second_out, step_out):
+    moment_new, second_new, update = lamb_moments(
+        gradient[...], divisor[:1, :1], weight[...], moment[...], second[...]
+    )
+    moment_out[...] = moment_new
+    second_out[...] = second_new
+    step_out[...] = trust[:, :1] * update
+
+
 def kernel_shards(n_dp, n_tensor, attn_out, grad_out, grad_acc, master_weight, moment_m, moment_v):
     tokens, columns = attn_out.shape
     rows_all = grad_out.shape[1]
@@ -245,12 +252,12 @@
     items = line * CHUNKS
     dma = pltpu.SemaphoreType.DMA
     whole = lambda: pltpu.VMEM((rows, columns), f32)
-    out = jax.ShapeDtypeStruct((rows, columns), f32)
-    return pl.pallas_call(
+    out = lambda height, width: jax.ShapeDtypeStruct((height, width), f32)
+    gradient, divisor, trust = pl.pallas_call(
         functools.partial(lamb_kernel, n_dp, n_tensor, rows_all * columns * n_tensor),
-        out_shape=(out, out, out),
-        in_specs=[pl.BlockSpec(memory_space=pl.ANY)] * 6,
-        out_specs=[pl.BlockSpec(memory_space=pl.ANY)] * 3,
+        out_shape=(out(rows, columns), out(8, LANES), out(rows, LANES)),
+        in_specs=[pl.BlockSpec(memory_space=pltpu.HBM)] * 6,
+        out_specs=[pl.BlockSpec(memory_space=pltpu.HBM)] * 3,
         scratch_shapes=[
             pltpu.VMEM((CHUNKS, tokens, width), jnp.bfloat16),
             pltpu.VMEM((tokens, rows_all), jnp.bfloat16),
@@ -259,7 +266,7 @@
             pltpu.VMEM((line, CHUNKS, rows, width), f32),
             pltpu.VMEM((line, CHUNKS, rows, width), f32),
             pltpu.VMEM((line, CHUNKS, rows, width), f32),
-            whole(), whole(), whole(), whole(), whole(), whole(), whole(), whole(),
+            whole(), whole(), whole(), whole(), whole(), pltpu.VMEM((8, LANES), f32), pltpu.VMEM((rows, LANES), f32),
             pltpu.VMEM((n_tensor, rows, LANES), f32),
             pltpu.VMEM((n_tensor, rows, LANES), f32),
             pltpu.VMEM((n_dp, 8, LANES), f32),
@@ -270,10 +277,18 @@
             dma((n_dp,)), dma((n_dp,)), dma((n_tensor,)), dma((n_tensor,)),
         ],
         compiler_params=pltpu.CompilerParams(
-            collective_id=0, has_side_effects=True, vmem_limit_bytes=40 * 2**20
+            collective_id=0, has_side_effects=True, vmem_limit_bytes=56 * 2**20
         ),
         name="lamb_step",
     )(attn_out, grad_out, grad_acc, master_weight, moment_m, moment_v)
+    return pl.pallas_call(
+        result_kernel,
+        out_shape=(out(rows, columns),) * 3,
+        in_specs=[pl.BlockSpec(memory_space=pltpu.VMEM)] * 6,
+        out_specs=[pl.BlockSpec(memory_space=pltpu.VMEM)] * 3,
+        compiler_params=pltpu.CompilerParams(vmem_limit_bytes=8 * 2**20),
+        name="results",
+    )(gradient, divisor, trust, master_weight, moment_m, moment_v)
 
 
 def collective_shards(n_dp, n_tensor, attn_out, grad_out, grad_acc, master_weight, moment_m, moment_v):

time: 51.4 us -> 45.3 us (0.88)
  local copies, waits for them, and re-layouts: 9.13 us -> 2.35 us
  Pallas kernels: 41.3 us -> 42 us
    unnamed x15 -> x12, local copies, waits for them, and re-layouts: 9.13 us -> 2.35 us
    pallas_call x0 -> x1, Pallas kernels: none -> 1 us  [kernel_shards(): pl.pallas_call(result_kernel, out_shape=(out(rows, columns),) * 3, in_spe...]
where the time goes in v2:
time: 45.3 us; the launch traced here: 45 us
  Pallas kernels  42 us (93%)
  local copies, waits for them, and re-layouts  2.35 us (5%)
  between operations  0.7 us (2%)
    pallas_call x1, Pallas kernels, kernel_shards(): pl.pallas_call(functools.partial(lamb_kernel, n_dp, n_tensor, rows_all *...  41 us
    unnamed x12, local copies, waits for them, and re-layouts  2.35 us
    pallas_call x1, Pallas kernels, kernel_shards(): pl.pallas_call(result_kernel, out_shape=(out(rows, columns),) * 3, in_spe...  1 us

profile of v2, /device:TPU:0, one launch (start us, length us, event | category | flops | bytes accessed | tf_op | source)
XLA Modules:
  0.0 45.0 jit_solution(910814931994175114)
XLA Ops:
  0.6 0.0 copy-start.2
  0.6 0.0 copy-start.1
  0.7 0.0 copy-start
  0.7 41.0 %lamb_step.1 = (f32[32,2048]{1,0:T(8,128)}, f32[8,128]{1,0:T(8,128)}, f32[32,128]{1,0:T(8,128)}) custom-call(bf16[1024,2048]{1,0:T(8,128)(2,1)} %attn.1, bf16[1024,256]{1,0:T(8,128)(2,1)} %grad_out.1, f32[32,2048]{1,0:T(8,128)} %grad_acc.1, f32[32,2048]{1,0:T(8,128)} %weight.3, f32[32,2048]{1,0:T(8,128)} %moment.3, f32[32,2048]{1,0:T(8,128)} %second.3), custom_call_target="tpu_custom_call" | custom-call | tf_op jit(solution)/shard_map/lamb_step/pallas_call | solution.py:256
  41.7 0.0 copy-done.2
  41.7 0.0 copy-done.1
  41.7 0.0 copy-done
  41.7 0.0 copy-start.3
  41.7 0.9 %copy-done.3 = f32[32,2048]{1,0:T(8,128)S(1)} copy-done((f32[32,2048]{1,0:T(8,128)S(1)}, f32[32,2048]{1,0:T(8,128)}, u32[]{:S(2)}) %copy-start.3) | copy-done | bytes 262168
  42.7 0.0 copy-start.4
  42.7 0.7 %copy-done.4 = f32[32,128]{1,0:T(8,128)S(1)} copy-done((f32[32,128]{1,0:T(8,128)S(1)}, f32[32,128]{1,0:T(8,128)}, u32[]{:S(2)}) %copy-start.4) | copy-done | bytes 16408
  43.4 0.0 copy-start.5
  43.4 0.7 %copy-done.5 = f32[8,128]{1,0:T(8,128)S(1)} copy-done((f32[8,128]{1,0:T(8,128)S(1)}, f32[8,128]{1,0:T(8,128)}, u32[]{:S(2)}) %copy-start.5) | copy-done | bytes 4120
  44.0 1.0 %results.1 = (f32[32,2048]{1,0:T(8,128)}, f32[32,2048]{1,0:T(8,128)}, f32[32,2048]{1,0:T(8,128)}) custom-call(f32[32,2048]{1,0:T(8,128)S(1)} %copy-done.3, f32[8,128]{1,0:T(8,128)S(1)} %copy-done.5, f32[32,128]{1,0:T(8,128)S(1)} %copy-done.4, f32[32,2048]{1,0:T(8,128)S(1)} %copy-done, f32[32,2048]{1,0:T(8,128)S(1)} %copy-done.1, f32[32,2048]{1,0:T(8,128)S(1)} %copy-done.2), custom_call_target="tpu_custom_call" | custom-call | tf_op jit(solution)/shard_map/results/pallas_call | solution.py:284
Async XLA Ops:
  0.6 41.0 %copy-start.2 = (f32[32,2048]{1,0:T(8,128)S(1)}, f32[32,2048]{1,0:T(8,128)}, u32[]{:S(2)}) copy-start(f32[32,2048]{1,0:T(8,128)} %second.3) | copy-start | bytes 786436
  0.6 41.0 %copy-start.1 = (f32[32,2048]{1,0:T(8,128)S(1)}, f32[32,2048]{1,0:T(8,128)}, u32[]{:S(2)}) copy-start(f32[32,2048]{1,0:T(8,128)} %moment.3) | copy-start | bytes 786436
  0.7 41.0 %copy-start = (f32[32,2048]{1,0:T(8,128)S(1)}, f32[32,2048]{1,0:T(8,128)}, u32[]{:S(2)}) copy-start(f32[32,2048]{1,0:T(8,128)} %weight.3) | copy-start | bytes 786436
  41.7 1.0 %copy-start.3 = (f32[32,2048]{1,0:T(8,128)S(1)}, f32[32,2048]{1,0:T(8,128)}, u32[]{:S(2)}) copy-start(f32[32,2048]{1,0:T(8,128)} %get-tuple-element.6.gradient) | copy-start | bytes 786436
  42.7 0.7 %copy-start.4 = (f32[32,128]{1,0:T(8,128)S(1)}, f32[32,128]{1,0:T(8,128)}, u32[]{:S(2)}) copy-start(f32[32,128]{1,0:T(8,128)} %get-tuple-element.8.trust) | copy-start | bytes 49156
  43.4 0.7 %copy-start.5 = (f32[8,128]{1,0:T(8,128)S(1)}, f32[8,128]{1,0:T(8,128)}, u32[]{:S(2)}) copy-start(f32[8,128]{1,0:T(8,128)} %get-tuple-element.7.divisor) | copy-start | bytes 12292

commit v3 on v2

--- a/solution.py
+++ b/solution.py
@@ -13,8 +13,8 @@
 epsilon = 1e-06
 
 MESH = pl.DeviceIdType.MESH
-CHUNKS = 4
-AHEAD = 4
+CHUNKS = 8
+AHEAD = 8
 LANES = 128
 MAX_LINE = 4
 
@@ -41,8 +41,15 @@
             group.append(left.pop(0))
             if right and len(right) > len(left):
                 group.append(right.pop(0))
-        order += [(place, chunk) for chunk in range(CHUNKS) for place in group]
-    return order + [(at, chunk) for chunk in range(CHUNKS)]
+        order += [(place, chunk) for chunk in range(1, CHUNKS) for place in group]
+    return order + [(at, chunk) for chunk in range(1, CHUNKS)]
+
+
+def line_first_steps(at, line):
+    right = [(to, 4 * at + 2 * (line - 1 - to)) for to in range(line - 1, at, -1)]
+    left = [(to, 4 * (line - 1 - at) + 2 * to) for to in range(at)]
+    own = max(4 * at + 2 * (line - 1 - at), 4 * (line - 1 - at) + 2 * at) + 2
+    return sorted(right + left, key=lambda step: step[1]) + [(at, own)]
 
 
 def lane_sums(values):
@@ -62,9 +69,10 @@
 def lamb_kernel(
     n_dp, n_tensor, entry_count,
     attn, grad_out, grad_acc, weight, moment, second,
-    grad_out_ref, divisor_out, trust_out,
+    grad_out_ref, stats_out,
     a_buf, g_buf, gt_buf, part, pair_in, from_left, from_right,
-    acc_buf, w_buf, m_buf, v_buf, grad_buf, div_buf, trust_buf,
+    first, first_pair, first_left, first_right,
+    acc_buf, w_buf, m_buf, v_buf, grad_buf, stats,
     wsum, usum, esum, tsum,
     load_sem, out_sem,
     pair_send, pair_recv, right_send, right_recv, left_send, left_recv,
@@ -77,10 +85,12 @@
     width = part.shape[3]
 
     loads = [pltpu.make_async_copy(grad_out, g_buf, load_sem.at[0])]
-    for c in range(CHUNKS):
-        loads.append(
-            pltpu.make_async_copy(attn.at[:, pl.ds(c * width, width)], a_buf.at[c], load_sem.at[1 + c])
-        )
+    chunk_order = [1, 0] + list(range(2, CHUNKS))
+    a_loads = [
+        pltpu.make_async_copy(attn.at[:, pl.ds(c * width, width)], a_buf.at[c], load_sem.at[1 + c])
+        for c in chunk_order
+    ]
+    loads += a_loads
     for i, (src, dst) in enumerate(((weight, w_buf), (grad_acc, acc_buf), (moment, m_buf), (second, v_buf))):
         loads.append(pltpu.make_async_copy(src, dst, load_sem.at[1 + CHUNKS + i]))
     for copy in loads:
@@ -114,6 +124,42 @@
             device_id=(dp + 2 * step, tensor), device_id_type=MESH,
         )
 
+    def first_line_copy(to, step):
+        i = to * CHUNKS
+        into, send, recv = (first_left, right_send, right_recv) if step > 0 else (first_right, left_send, left_recv)
+        return pltpu.make_async_remote_copy(
+            src_ref=first.at[to], dst_ref=into.at[to], send_sem=send.at[i], recv_sem=recv.at[i],
+            device_id=(dp + 2 * step, tensor), device_id_type=MESH,
+        )
+
+    def first_pair_copy(at):
+        return pltpu.make_async_remote_copy(
+            src_ref=first.at[at, 1 - side], dst_ref=first_pair,
+            send_sem=pair_send.at[at * CHUNKS], recv_sem=pair_recv.at[at * CHUNKS],
+            device_id=(2 * place + (1 - side), tensor), device_id_type=MESH,
+        )
+
+    def first_step(at, to):
+        if to == at:
+            total = first[at]
+            if at > 0:
+                first_line_copy(at, 1).wait_recv()
+                total = total + first_left[at]
+            if at < line - 1:
+                first_line_copy(at, -1).wait_recv()
+                total = total + first_right[at]
+            first[at] = total
+            first_pair_copy(at).start()
+            return
+        step = 1 if to > at else -1
+        if step > 0 and at > 0:
+            first_line_copy(to, 1).wait_recv()
+            first[to] = first[to] + first_left[to]
+        if step < 0 and at < line - 1:
+            first_line_copy(to, -1).wait_recv()
+            first[to] = first[to] + first_right[to]
+        first_line_copy(to, step).start()
+
     def tensor_copy(k, src, dst, send, recv):
         return pltpu.make_async_remote_copy(
             src_ref=src, dst_ref=dst.at[k], send_sem=send.at[k], recv_sem=recv.at[k],
@@ -130,11 +176,14 @@
     gt_buf[...] = g_buf[...].T
 
     orders = [block_order(at, line) for at in range(line)]
-    for c in range(CHUNKS):
-        loads[1 + c].wait()
+    for n, c in enumerate(chunk_order):
+        a_loads[n].wait()
         product = jnp.dot(gt_buf[...], a_buf[c], preferred_element_type=jnp.float32)
-        part[:, c] = product.reshape(n_dp, product.shape[0] // n_dp, width)
         if c == 0:
+            first[...] = product.reshape(first.shape)
+        else:
+            part[:, c] = product.reshape(n_dp, product.shape[0] // n_dp, width)
+        if n == 0:
             pl.semaphore_wait(barrier, n_dp + n_tensor - 2)
         for at in range(line):
             @pl.when(place == at)
@@ -142,6 +191,9 @@
                 for item in orders[at][:AHEAD]:
                     if item[1] == c:
                         pair_copy(item).start()
+                if c == 0 and at in (0, line - 1):
+                    for to, _ in line_first_steps(at, line)[:-1]:
+                        first_step(at, to)
 
     loads[1 + CHUNKS].wait()
     wsum[0] = lane_sums(jnp.square(w_buf[...]))
@@ -156,8 +208,19 @@
         def _(at=at):
             order = orders[at]
             energy = jnp.zeros((8, LANES), jnp.float32)
+            early = line_first_steps(at, line)
+            if at in (0, line - 1):
+                early = early[-1:]
             for i, item in enumerate(order):
                 to, c = item
+                for early_to, when in early:
+                    if when == i:
+                        first_step(at, early_to)
+                if i == len(order) - 4:
+                    first_pair_copy(at).wait_recv()
+                    total = first[at, side] + first_pair[...] + acc_buf[:, :width]
+                    grad_buf[:, :width] = total
+                    energy = energy + row_groups(lane_sums(jnp.square(total)))
                 pair_copy(item).wait_recv()
                 if i + AHEAD < len(order):
                     pair_copy(order[i + AHEAD]).start()
@@ -179,8 +242,7 @@
 
     outs = [
         pltpu.make_async_copy(grad_buf, grad_out_ref, out_sem.at[0]),
-        pltpu.make_async_copy(div_buf, divisor_out, out_sem.at[1]),
-        pltpu.make_async_copy(trust_buf, trust_out, out_sem.at[2]),
+        pltpu.make_async_copy(stats, stats_out, out_sem.at[1]),
     ]
     t_copies = [tensor_copy(k, tsum.at[0], tsum, t_send, t_recv) for k in range(1, n_tensor)]
     for copy in t_copies:
@@ -200,8 +262,7 @@
     mean_square = jnp.sum(energy, keepdims=True) * (1.0 / entry_count)
     divisor = jnp.sqrt(mean_square + epsilon)
 
-    div_buf[...] = jnp.broadcast_to(divisor, div_buf.shape)
-    outs[1].start()
+    stats[:8] = jnp.broadcast_to(divisor, (8, LANES))
     update = lamb_moments(grad_buf[...], divisor, w_buf[...], m_buf[...], v_buf[...])[2]
     usum[0] = lane_sums(update * update)
     u_copies = [tensor_copy(k, usum.at[0], usum, u_send, u_recv) for k in range(1, n_tensor)]
@@ -217,14 +278,18 @@
         copy.wait_recv()
         update_square = update_square + usum[k + 1]
     update_norm = jnp.sqrt(jnp.sum(update_square, axis=1, keepdims=True))
-    trust_buf[...] = jnp.broadcast_to(weight_norm / (update_norm + epsilon), trust_buf.shape)
-    outs[2].start()
+    stats[8:] = jnp.broadcast_to(weight_norm / (update_norm + epsilon), (stats.shape[0] - 8, LANES))
+    outs[1].start()
 
     for copy in w_copies + t_copies + e_copies + u_copies:
         copy.wait_send()
     for at in range(line):
         @pl.when(place == at)
         def _(at=at):
+            first_pair_copy(at).wait_send()
+            for to in range(line):
+                if to != at:
+                    first_line_copy(to, 1 if to > at else -1).wait_send()
             for item in orders[at]:
                 pair_copy(item).wait_send()
                 if item[0] != at:
@@ -233,13 +298,20 @@
         copy.wait()
 
 
-def result_kernel(gradient, divisor, trust, weight, moment, second, moment_out, second_out, step_out):
+def result_kernel(*refs):
+    sources, (moment_out, second_out, step_out), buffers, sem = refs[:5], refs[5:8], refs[8:13], refs[13]
+    loads = [pltpu.make_async_copy(src, dst, sem.at[i]) for i, (src, dst) in enumerate(zip(sources, buffers))]
+    for copy in loads:
+        copy.start()
+    for copy in loads:
+        copy.wait()
+    gradient, stats, weight, moment, second = buffers
     moment_new, second_new, update = lamb_moments(
-        gradient[...], divisor[:1, :1], weight[...], moment[...], second[...]
+        gradient[...], stats[:1, :1], weight[...], moment[...], second[...]
     )
     moment_out[...] = moment_new
     second_out[...] = second_new
-    step_out[...] = trust[:, :1] * update
+    step_out[...] = stats[8:, :1] * update
 
 
 def kernel_shards(n_dp, n_tensor, attn_out, grad_out, grad_acc, master_weight, moment_m, moment_v):
@@ -253,11 +325,11 @@
     dma = pltpu.SemaphoreType.DMA
     whole = lambda: pltpu.VMEM((rows, columns), f32)
     out = lambda height, width: jax.ShapeDtypeStruct((height, width), f32)
-    gradient, divisor, trust = pl.pallas_call(
+    gradient, stats = pl.pallas_call(
         functools.partial(lamb_kernel, n_dp, n_tensor, rows_all * columns * n_tensor),
-        out_shape=(out(rows, columns), out(8, LANES), out(rows, LANES)),
+        out_shape=(out(rows, columns), out(8 + rows, LANES)),
         in_specs=[pl.BlockSpec(memory_space=pltpu.HBM)] * 6,
-        out_specs=[pl.BlockSpec(memory_space=pltpu.HBM)] * 3,
+        out_specs=[pl.BlockSpec(memory_space=pltpu.HBM)] * 2,
         scratch_shapes=[
             pltpu.VMEM((CHUNKS, tokens, width), jnp.bfloat16),
             pltpu.VMEM((tokens, rows_all), jnp.bfloat16),
@@ -266,12 +338,16 @@
             pltpu.VMEM((line, CHUNKS, rows, width), f32),
             pltpu.VMEM((line, CHUNKS, rows, width), f32),
             pltpu.VMEM((line, CHUNKS, rows, width), f32),
-            whole(), whole(), whole(), whole(), whole(), pltpu.VMEM((8, LANES), f32), pltpu.VMEM((rows, LANES), f32),
+            pltpu.VMEM((line, 2, rows, width), f32),
+            pltpu.VMEM((rows, width), f32),
+            pltpu.VMEM((line, 2, rows, width), f32),
+            pltpu.VMEM((line, 2, rows, width), f32),
+            whole(), whole(), whole(), whole(), whole(), pltpu.VMEM((8 + rows, LANES), f32),
             pltpu.VMEM((n_tensor, rows, LANES), f32),
             pltpu.VMEM((n_tensor, rows, LANES), f32),
             pltpu.VMEM((n_dp, 8, LANES), f32),
             pltpu.VMEM((n_tensor, 8, LANES), f32),
-            dma((CHUNKS + 5,)), dma((3,)),
+            dma((CHUNKS + 5,)), dma((2,)),
             dma((items,)), dma((items,)), dma((items,)), dma((items,)), dma((items,)), dma((items,)),
             dma((n_tensor,)), dma((n_tensor,)), dma((n_tensor,)), dma((n_tensor,)),
             dma((n_dp,)), dma((n_dp,)), dma((n_tensor,)), dma((n_tensor,)),
@@ -284,11 +360,12 @@
     return pl.pallas_call(
         result_kernel,
         out_shape=(out(rows, columns),) * 3,
-        in_specs=[pl.BlockSpec(memory_space=pltpu.VMEM)] * 6,
+        in_specs=[pl.BlockSpec(memory_space=pltpu.HBM)] * 5,
         out_specs=[pl.BlockSpec(memory_space=pltpu.VMEM)] * 3,
-        compiler_params=pltpu.CompilerParams(vmem_limit_bytes=8 * 2**20),
+        scratch_shapes=[whole(), pltpu.VMEM((8 + rows, LANES), f32), whole(), whole(), whole(), dma((5,))],
+        compiler_params=pltpu.CompilerParams(vmem_limit_bytes=56 * 2**20),
         name="results",
-    )(gradient, divisor, trust, master_weight, moment_m, moment_v)
+    )(gradient, stats, master_weight, moment_m, moment_v)
 
 
 def collective_shards(n_dp, n_tensor, attn_out, grad_out, grad_acc, master_weight, moment_m, moment_v):

time: 45.3 us -> 44.8 us (0.989)
  local copies, waits for them, and re-layouts: 2.35 us -> 0 us
  Pallas kernels: 42 us -> 44.1 us
    unnamed x12 -> x0, local copies, waits for them, and re-layouts: 2.35 us -> none
    pallas_call x1, Pallas kernels: 1 us -> 2.26 us  [kernel_shards(): pl.pallas_call(result_kernel, out_shape=(out(rows, columns),) * 3, in_spe...]
    pallas_call x1, Pallas kernels: 41 us -> 41.8 us  [kernel_shards(): pl.pallas_call(functools.partial(lamb_kernel, n_dp, n_tensor, rows_all *...]
where the time goes in v3:
time: 44.8 us; the launch traced here: 44.7 us
  Pallas kernels  44.1 us (98%)
  between operations  0.64 us (1%)
    pallas_call x1, Pallas kernels, kernel_shards(): pl.pallas_call(functools.partial(lamb_kernel, n_dp, n_tensor, rows_all *...  41.8 us
    pallas_call x1, Pallas kernels, kernel_shards(): pl.pallas_call(result_kernel, out_shape=(out(rows, columns),) * 3, in_spe...  2.26 us

profile of v3, /device:TPU:0, one launch (start us, length us, event | category | flops | bytes accessed | tf_op | source)
XLA Modules:
  0.0 44.7 jit_solution(11574875919444495040)
XLA Ops:
  0.6 41.8 %lamb_step.1 = (f32[32,2048]{1,0:T(8,128)}, f32[40,128]{1,0:T(8,128)}) custom-call(bf16[1024,2048]{1,0:T(8,128)(2,1)} %attn.1, bf16[1024,256]{1,0:T(8,128)(2,1)} %grad_out.1, f32[32,2048]{1,0:T(8,128)} %grad_acc.1, f32[32,2048]{1,0:T(8,128)} %refs_2_.1, f32[32,2048]{1,0:T(8,128)} %refs_3_.1, f32[32,2048]{1,0:T(8,128)} %refs_4_.1), custom_call_target="tpu_custom_call" | custom-call | tf_op jit(solution)/shard_map/lamb_step/pallas_call | solution.py:328
  42.4 2.3 %results.1 = (f32[32,2048]{1,0:T(8,128)}, f32[32,2048]{1,0:T(8,128)}, f32[32,2048]{1,0:T(8,128)}) custom-call(f32[32,2048]{1,0:T(8,128)} %get-tuple-element.5.refs_0_, f32[40,128]{1,0:T(8,128)} %get-tuple-element.6.refs_1_, f32[32,2048]{1,0:T(8,128)} %refs_2_.1, f32[32,2048]{1,0:T(8,128)} %refs_3_.1, f32[32,2048]{1,0:T(8,128)} %refs_4_.1), custom_call_target="tpu_custom_call" | custom-call | tf_op jit(solution)/shard_map/results/pallas_call | solution.py:360
